TPU v7x, 32 devices: a whole 2x2x4 slice. The times are simulated.
32 devices in a mesh: node: 8 (over z, y), local: 4 (over x, core).
Axes of the slice: x: 2, y: 2, z: 4, core: 2. Of those that a mesh axis runs over, the one named last changes fastest.
Arguments:
- tok_x: bfloat16 [64, 2048], P(('node', 'local')), may hold values from -6 to 6
- grad_out: bfloat16 [64, 2048], P(('node', 'local')), may hold values from -6 to 6
- expert_ids: int32 [64, 8], P('node'), may hold values from 0 to 31, as said below
- slot_ids: int32 [64, 8], P('node'), may hold values from 0 to 7, as said below
- route_probs: bfloat16 [64, 8], P('node'), may hold values from 0.099609375 to 1
- gate_weight: bfloat16 [32, 768, 2048], P(('node', 'local')), may hold values from -0.125 to 0.125
- up_weight: bfloat16 [32, 768, 2048], P(('node', 'local')), may hold values from -0.125 to 0.125
- down_weight: bfloat16 [32, 768, 2048], P(('node', 'local')), may hold values from -0.21875 to 0.21875
Outputs:
- grad_x: bfloat16 [64, 2048], P(('node', 'local'))
- grad_probs: float32 [64, 8], P(('node', 'local'))
- grad_gate: float32 [32, 768, 2048], P(('node', 'local'))
- grad_up: float32 [32, 768, 2048], P(('node', 'local'))
- grad_down: float32 [32, 768, 2048], P(('node', 'local'))
Inputs may be any that keep to these rules, and one draw needn't show every extreme that they name: `expert_ids`: each token names 8 different experts. Among the 8 tokens of every index of node, some expert is named by all 8 tokens. `slot_ids`: the pairs of the 8 tokens of one index of node that name one expert carry the slots 0, 1, 2 and so on, each once.
All inputs are finite; a program needn't handle non-finite values.
Results may differ from a plain program's by a relative error of at most 0.0049.
Values may be sent and summed in bfloat16 or wider, within the bound.
A program may use at most 64 MiB of HBM per device.

v0:
```python
import jax
import jax.numpy as jnp
from jax import lax
from jax.sharding import PartitionSpec as P

EXP_NODE = 4
CAPN = 7


contract_last = (((1,), (1,)), ((), ()))
contract_first = (((0,), (0,)), ((), ()))


def owner_grads(owner_x, owner_d, owner_p, w_gate_rows, w_up_rows, w_down_rows):
    gate_pre = lax.dot_general(
        owner_x, w_gate_rows, contract_last, preferred_element_type=jnp.float32
    )
    up_pre = lax.dot_general(owner_x, w_up_rows, contract_last, preferred_element_type=jnp.float32)
    sigmoid_gate = jax.nn.sigmoid(gate_pre)
    activated = gate_pre * sigmoid_gate
    hidden = activated * up_pre
    back_proj = lax.dot_general(
        owner_d, w_down_rows, contract_last, preferred_element_type=jnp.float32
    )
    pair_grad = jnp.sum(hidden * back_proj, axis=1)
    d_hidden = owner_p[:, None] * back_proj
    d_gate = (d_hidden * up_pre * sigmoid_gate * (1.0 + gate_pre * (1.0 - sigmoid_gate))).astype(
        jnp.bfloat16
    )
    d_up = (d_hidden * activated).astype(jnp.bfloat16)
    scaled_hidden = (owner_p[:, None] * hidden).astype(jnp.bfloat16)
    input_grad = jnp.dot(d_gate, w_gate_rows, preferred_element_type=jnp.float32) + jnp.dot(
        d_up, w_up_rows, preferred_element_type=jnp.float32
    )
    gate_grad = lax.dot_general(d_gate, owner_x, contract_first, preferred_element_type=jnp.float32)
    up_grad = lax.dot_general(d_up, owner_x, contract_first, preferred_element_type=jnp.float32)
    down_grad = lax.dot_general(
        scaled_hidden, owner_d, contract_first, preferred_element_type=jnp.float32
    )
    return (input_grad, pair_grad, gate_grad, up_grad, down_grad)


def local(tok_x, grad_out, expert_ids, slot_ids, route_probs, gate_weight, up_weight, down_weight):
    node_count = lax.axis_size("node")
    owners = lax.axis_size("local") // EXP_NODE
    place = lax.axis_index("local")
    own_class = place // owners
    node_tokens = expert_ids.shape[0]
    top_count = expert_ids.shape[1]
    model_width = tok_x.shape[1]
    pair_count = node_tokens * top_count
    node_x, node_d = (
        lax.all_gather(tok_x, "local", axis=0, tiled=True),
        lax.all_gather(grad_out, "local", axis=0, tiled=True),
    )
    flat_expert = expert_ids.reshape(-1)
    flat_slot = slot_ids.reshape(-1)
    pair_ids = jnp.arange(pair_count, dtype=jnp.int32)
    is_mine = (flat_expert % EXP_NODE == own_class) & (flat_slot < CAPN)
    target = jnp.where(is_mine, flat_expert // EXP_NODE * CAPN + flat_slot, node_count * CAPN)
    slot_table = (
        jnp.full((node_count * CAPN,), pair_count, jnp.int32).at[target].set(pair_ids, mode="drop")
    )
    token_rows = slot_table // top_count
    outbox_p = jnp.take(route_probs.reshape(-1), slot_table, mode="fill", fill_value=0).reshape(
        node_count, CAPN
    )
    outbox_x = jnp.take(node_x, token_rows, axis=0, mode="fill", fill_value=0).reshape(
        node_count, CAPN, model_width
    )
    outbox_d = jnp.take(node_d, token_rows, axis=0, mode="fill", fill_value=0).reshape(
        node_count, CAPN, model_width
    )
    arrived_x, arrived_d, arrived_p = (
        lax.all_to_all(outbox_x, "node", split_axis=0, concat_axis=0, tiled=True),
        lax.all_to_all(outbox_d, "node", split_axis=0, concat_axis=0, tiled=True),
        lax.all_to_all(outbox_p, "node", split_axis=0, concat_axis=0, tiled=True),
    )
    owner_x = arrived_x.reshape(-1, model_width)
    owner_d = arrived_d.reshape(-1, model_width)
    owner_p = arrived_p.reshape(-1).astype(jnp.float32)
    input_grad, pair_grad, gate_grad, up_grad, down_grad = owner_grads(
        owner_x, owner_d, owner_p, gate_weight[0], up_weight[0], down_weight[0]
    )
    token_hits = (token_rows[None, :] == jnp.arange(node_tokens, dtype=jnp.int32)[:, None]).astype(
        jnp.float32
    )
    back_x, back_p = (
        lax.all_to_all(
            input_grad.reshape(node_count, CAPN, model_width),
            "node",
            split_axis=0,
            concat_axis=0,
            tiled=True,
        ),
        lax.all_to_all(
            pair_grad.reshape(node_count, CAPN), "node", split_axis=0, concat_axis=0, tiled=True
        ),
    )
    token_x = jnp.dot(
        token_hits,
        back_x.reshape(-1, model_width),
        precision=lax.Precision.HIGHEST,
        preferred_element_type=jnp.float32,
    )
    token_p = (
        jnp.zeros((pair_count,), jnp.float32)
        .at[slot_table]
        .add(back_p.reshape(-1), mode="drop")
        .reshape(node_tokens, top_count)
    )
    summed_x, summed_p = (
        lax.psum_scatter(token_x, "local", scatter_dimension=0, tiled=True),
        lax.psum_scatter(token_p, "local", scatter_dimension=0, tiled=True),
    )
    return (
        summed_x.astype(jnp.bfloat16),
        summed_p,
        gate_grad[None],
        up_grad[None],
        down_grad[None],
    )


def solution(mesh):
    in_specs = (
        P(("node", "local"), None),
        P(("node", "local"), None),
        P("node", None),
        P("node", None),
        P("node", None),
        P(("node", "local"), None, None),
        P(("node", "local"), None, None),
        P(("node", "local"), None, None),
    )
    out_specs = (
        P(("node", "local"), None),
        P(("node", "local"), None),
        P(("node", "local"), None, None),
        P(("node", "local"), None, None),
        P(("node", "local"), None, None),
    )
    return jax.shard_map(local, mesh=mesh, in_specs=in_specs, out_specs=out_specs, check_vma=False)
```

profile of v0, /device:TPU:0, one launch (start us, length us, event | category | flops | bytes accessed | tf_op | source)
XLA Modules:
  0.0 111.8 jit_solution(9568913968246403817)
XLA Ops:
  6.0 7.3 %all-to-all-start = ((bf16[8,1,7]{2,1,0:T(2,128)(2,1)}), bf16[8,1,7]{2,1,0:T(2,128)(2,1)S(1)}, u32[]{:S(2)}, u32[]{:S(2)}) async-start(bf16[8,1,7]{2,1,0:T(2,128)(2,1)} %select_n.94), calls=%async_computation | async-start | bytes 8192 | tf_op jit(solution)/shard_map/all_to_all | solution.py:77
  13.8 5.4 %all-gather.1 = bf16[4,2,2048]{2,1,0:T(2,128)(2,1)S(1)} all-gather(bf16[1,2,2048]{2,1,0:T(2,128)(2,1)} %bitcast.41), channel_id=1, replica_groups=mesh['node'=8,'local'=4] {'local'}, dimensions={0}, use_global_device_ids=true | all-gather | bytes 40960 | tf_op jit(solution)/shard_map/all_gather | solution.py:53
  19.2 5.4 %all-gather = bf16[4,2,2048]{2,1,0:T(2,128)(2,1)S(1)} all-gather(bf16[1,2,2048]{2,1,0:T(2,128)(2,1)} %bitcast.42), channel_id=1, replica_groups=mesh['node'=8,'local'=4] {'local'}, dimensions={0}, use_global_device_ids=true | all-gather | bytes 40960 | tf_op jit(solution)/shard_map/all_gather | solution.py:54
  25.3 1.4 %gather_fusion.2 = bf16[56,2048]{1,0:T(8,128)(2,1)} fusion(bf16[8,2048]{1,0:T(8,128)(2,1)S(1)} %reshape.286, s32[1024]{0:T(1024)S(1)} %pad_clamp_fusion), kind=kCustom, calls=%fused_computation.1.clone | custom fusion | bytes 458976 | tf_op jit(solution)/shard_map/jit(_take)/gather | solution.py:68
  26.8 1.8 %broadcast_select_fusion.1 = (bf16[56,2048]{1,0:T(8,128)(2,1)}, bf16[56,2048]{1,0:T(8,128)(2,1)}) fusion(bf16[56,2048]{1,0:T(8,128)(2,1)S(1)} %gather_fusion.1, pred[56]{0:T(512)(128)(4,1)S(1)} %get-tuple-element.8, bf16[56,2048]{1,0:T(8,128)(2,1)} %gather_fusion.2), kind=kLoop, calls=%fused_computation.20 | loop fusion | flops 229376 | bytes 917560 | tf_op jit(solution)/shard_map/jit(_take)/select_n | solution.py:71
  28.6 1.7 %reshape.232 = bf16[8,7,2048]{2,1,0:T(8,128)(2,1)} reshape(bf16[56,2048]{1,0:T(8,128)(2,1)} %get-tuple-element.14) | data formatting | bytes 458752 | tf_op jit(solution)/shard_map/reshape | solution.py:68
  30.3 6.0 %all-to-all-start.2 = ((bf16[8,7,2048]{2,1,0:T(8,128)(2,1)}), bf16[8,7,2048]{2,1,0:T(8,128)(2,1)S(1)}, u32[]{:S(2)}, u32[]{:S(2)}) async-start(bf16[8,7,2048]{2,1,0:T(8,128)(2,1)} %reshape.232), calls=%async_computation.2 | async-start | bytes 524288 | tf_op jit(solution)/shard_map/all_to_all | solution.py:75
  36.3 1.7 %reshape.230 = bf16[8,7,2048]{2,1,0:T(8,128)(2,1)} reshape(bf16[56,2048]{1,0:T(8,128)(2,1)} %get-tuple-element.13) | data formatting | bytes 458752 | tf_op jit(solution)/shard_map/reshape | solution.py:71
  38.1 7.6 %all-to-all-done.2 = bf16[8,7,2048]{2,1,0:T(8,128)(2,1)S(1)} async-done(((bf16[8,7,2048]{2,1,0:T(8,128)(2,1)}), bf16[8,7,2048]{2,1,0:T(8,128)(2,1)S(1)}, u32[]{:S(2)}, u32[]{:S(2)}) %all-to-all-start.2) | async-done | bytes 229408 | tf_op jit(solution)/shard_map/all_to_all | solution.py:75
  46.4 4.0 %all-to-all-start.1 = ((bf16[8,7,2048]{2,1,0:T(8,128)(2,1)}), bf16[8,7,2048]{2,1,0:T(8,128)(2,1)}, u32[]{:S(2)}, u32[]{:S(2)}) async-start(bf16[8,7,2048]{2,1,0:T(8,128)(2,1)} %reshape.230), calls=%async_computation.1 | async-start | bytes 524288 | tf_op jit(solution)/shard_map/all_to_all | solution.py:76
  53.4 1.8 %fusion.6 = f32[56,768]{1,0:T(8,128)} fusion(bf16[56,2048]{1,0:T(8,128)(2,1)S(1)} %reshape.233, bf16[1,768,2048]{2,1,0:T(8,128)(2,1)S(1)} %copy-done.1), kind=kOutput, calls=%fused_computation.14 | convolution fusion | flops 176160768 | bytes 3547136 | tf_op jit(solution)/shard_map/dot_general | solution.py:18
  55.1 3.9 %all-to-all-done.1 = bf16[8,7,2048]{2,1,0:T(8,128)(2,1)} async-done(((bf16[8,7,2048]{2,1,0:T(8,128)(2,1)}), bf16[8,7,2048]{2,1,0:T(8,128)(2,1)}, u32[]{:S(2)}, u32[]{:S(2)}) %all-to-all-start.1) | async-done | bytes 229408 | tf_op jit(solution)/shard_map/all_to_all | solution.py:76
  59.0 1.7 %reshape.231 = bf16[56,2048]{1,0:T(8,128)(2,1)} reshape(bf16[8,7,2048]{2,1,0:T(8,128)(2,1)} %all-to-all-done.1) | data formatting | bytes 458752 | tf_op jit(solution)/shard_map/reshape | solution.py:80
  60.8 3.8 %multiply_reduce_fusion = (f32[56]{0:T(128)S(1)}, bf16[56,768]{1,0:T(8,128)(2,1)}, bf16[56,768]{1,0:T(8,128)(2,1)}) fusion(f32[56,768]{1,0:T(8,128)} %fusion.6, f32[56,768]{1,0:T(8,128)S(1)} %fusion.2, f32[56]{0:T(128)S(1)} %reshape.238, bf16[56,2048]{1,0:T(8,128)(2,1)} %reshape.231, bf16[1,768,2048]{2,1,0:T(8,128)(2,1)} %param.17), kind=kOutput, calls=%fused_computation.22 | convolution fusion | flops 176891840 | bytes 3891648 | tf_op jit(solution)/shard_map/dot_general | solution.py:22
  65.3 3.6 %all-to-all-start.4 = ((f32[8,1,7]{2,1,0:T(1,128)}), f32[8,1,7]{2,1,0:T(1,128)S(1)}, u32[]{:S(2)}, u32[]{:S(2)}) async-start(f32[8,1,7]{2,1,0:T(1,128)} %bitcast.6), calls=%async_computation.4 | async-start | bytes 8192 | tf_op jit(solution)/shard_map/all_to_all | solution.py:96
  68.9 1.7 %fusion = f32[56,2048]{1,0:T(8,128)S(1)} fusion(bf16[56,768]{1,0:T(8,128)(2,1)} %get-tuple-element.11, bf16[1,768,2048]{2,1,0:T(8,128)(2,1)S(1)} %copy-done), kind=kOutput, calls=%fused_computation.8 | convolution fusion | flops 176160768 | bytes 3690496 | tf_op jit(solution)/shard_map/dot_general | solution.py:32
  70.8 1.4 %fusion.10 = f32[56,2048]{1,0:T(8,128)} fusion(f32[56,2048]{1,0:T(8,128)S(1)} %fusion, bf16[56,768]{1,0:T(8,128)(2,1)S(1)} %copy-done.5, bf16[1,768,2048]{2,1,0:T(8,128)(2,1)S(1)} %copy-done.2), kind=kOutput, calls=%fused_computation.18 | convolution fusion | flops 176275456 | bytes 4149248 | tf_op jit(solution)/shard_map/dot_general | solution.py:32
  72.2 1.9 %reshape.234 = f32[8,7,2048]{2,1,0:T(8,128)} reshape(f32[56,2048]{1,0:T(8,128)} %fusion.10) | data formatting | bytes 917504 | tf_op jit(solution)/shard_map/reshape | solution.py:90
  75.3 4.8 %all-to-all-start.3 = ((f32[8,7,2048]{2,1,0:T(8,128)}), f32[8,7,2048]{2,1,0:T(8,128)}, u32[]{:S(2)}, u32[]{:S(2)}) async-start(f32[8,7,2048]{2,1,0:T(8,128)} %reshape.234), calls=%async_computation.3 | async-start | bytes 1048576 | tf_op jit(solution)/shard_map/all_to_all | solution.py:89
  82.0 4.6 %convolution_bitcast_fusion.1 = f32[1,768,2048]{2,1,0:T(8,128)} fusion(bf16[56,768]{1,0:T(8,128)(2,1)} %get-tuple-element.12, bf16[56,2048]{1,0:T(8,128)(2,1)S(1)} %reshape.233), kind=kOutput, calls=%fused_computation.6 | convolution fusion | flops 176160768 | bytes 6606848 | tf_op jit(solution)/shard_map/dot_general | solution.py:36
  86.6 3.7 %convolution_bitcast_fusion.2 = f32[1,768,2048]{2,1,0:T(8,128)} fusion(bf16[56,768]{1,0:T(8,128)(2,1)S(1)} %copy-done.6, bf16[56,2048]{1,0:T(8,128)(2,1)S(1)} %reshape.233), kind=kOutput, calls=%fused_computation.7 | convolution fusion | flops 176160768 | bytes 6606848 | tf_op jit(solution)/shard_map/dot_general | solution.py:35
  90.3 3.8 %convolution_bitcast_fusion = f32[1,768,2048]{2,1,0:T(8,128)} fusion(bf16[56,2048]{1,0:T(8,128)(2,1)S(1)} %copy-done.4, f32[56]{0:T(128)S(1)} %reshape.238, f32[56,768]{1,0:T(8,128)S(1)} %copy-done.3, f32[56,768]{1,0:T(8,128)S(1)} %fusion.2), kind=kOutput, calls=%fused_computation.5 | convolution fusion | flops 176461824 | bytes 6865120 | tf_op jit(solution)/shard_map/dot_general | solution.py:37
  96.5 1.9 %reshape.235 = f32[56,2048]{1,0:T(8,128)} reshape(f32[8,7,2048]{2,1,0:T(8,128)} %all-to-all-done.3) | data formatting | bytes 917504 | tf_op jit(solution)/shard_map/reshape | solution.py:102
  99.7 10.9 %all-reduce.2 = (bf16[8,2048]{1,0:T(8,128)(2,1)S(1)}, f32[8,8]{1,0:T(8,128)S(1)}) all-reduce(f32[8,2048]{1,0:T(8,128)S(1)} %fusion.16, f32[8,8]{1,0:T(8,128)S(1)} %reshape.237), channel_id=2, replica_groups=mesh['node'=8,'local'=4] {'local'}, use_global_device_ids=true, to_apply=%region_1.3.clone | all-reduce | flops 16448 | bytes 98816
  (56 shorter events, 18.5 us)
Async XLA Ops:
  0.6 50.9 %copy-start = (bf16[1,768,2048]{2,1,0:T(8,128)(2,1)S(1)}, bf16[1,768,2048]{2,1,0:T(8,128)(2,1)}, u32[]{:S(2)}) copy-start(bf16[1,768,2048]{2,1,0:T(8,128)(2,1)} %param.15) | copy-start | bytes 9437188
  4.0 0.5 copy-start.10
  6.0 24.3 %all-to-all-start = ((bf16[8,1,7]{2,1,0:T(2,128)(2,1)}), bf16[8,1,7]{2,1,0:T(2,128)(2,1)S(1)}, u32[]{:S(2)}, u32[]{:S(2)}) async-start(bf16[8,1,7]{2,1,0:T(2,128)(2,1)} %select_n.94), calls=%async_computation | async-start | bytes 8192 | tf_op jit(solution)/shard_map/all_to_all | solution.py:77
  13.3 0.5 copy-start.8
  30.3 15.4 %all-to-all-start.2 = ((bf16[8,7,2048]{2,1,0:T(8,128)(2,1)}), bf16[8,7,2048]{2,1,0:T(8,128)(2,1)S(1)}, u32[]{:S(2)}, u32[]{:S(2)}) async-start(bf16[8,7,2048]{2,1,0:T(8,128)(2,1)} %reshape.232), calls=%async_computation.2 | async-start | bytes 524288 | tf_op jit(solution)/shard_map/all_to_all | solution.py:75
  45.7 0.7 copy-start.7
  46.4 12.7 %all-to-all-start.1 = ((bf16[8,7,2048]{2,1,0:T(8,128)(2,1)}), bf16[8,7,2048]{2,1,0:T(8,128)(2,1)}, u32[]{:S(2)}, u32[]{:S(2)}) async-start(bf16[8,7,2048]{2,1,0:T(8,128)(2,1)} %reshape.230), calls=%async_computation.1 | async-start | bytes 524288 | tf_op jit(solution)/shard_map/all_to_all | solution.py:76
  51.5 1.9 %copy-start.1 = (bf16[1,768,2048]{2,1,0:T(8,128)(2,1)S(1)}, bf16[1,768,2048]{2,1,0:T(8,128)(2,1)}, u32[]{:S(2)}) copy-start(bf16[1,768,2048]{2,1,0:T(8,128)(2,1)} %param.16) | copy-start | bytes 9437188
  65.3 10.0 %all-to-all-start.4 = ((f32[8,1,7]{2,1,0:T(1,128)}), f32[8,1,7]{2,1,0:T(1,128)S(1)}, u32[]{:S(2)}, u32[]{:S(2)}) async-start(f32[8,1,7]{2,1,0:T(1,128)} %bitcast.6), calls=%async_computation.4 | async-start | bytes 8192 | tf_op jit(solution)/shard_map/all_to_all | solution.py:96
  68.9 1.9 %copy-start.2 = (bf16[1,768,2048]{2,1,0:T(8,128)(2,1)S(1)}, bf16[1,768,2048]{2,1,0:T(8,128)(2,1)}, u32[]{:S(2)}) copy-start(bf16[1,768,2048]{2,1,0:T(8,128)(2,1)} %param.16) | copy-start | bytes 9437188
  68.9 1.9 %copy-start.5 = (bf16[56,768]{1,0:T(8,128)(2,1)S(1)}, bf16[56,768]{1,0:T(8,128)(2,1)}, u32[]{:S(2)}) copy-start(bf16[56,768]{1,0:T(8,128)(2,1)} %get-tuple-element.12) | copy-start | bytes 258052
  75.3 21.3 %all-to-all-start.3 = ((f32[8,7,2048]{2,1,0:T(8,128)}), f32[8,7,2048]{2,1,0:T(8,128)}, u32[]{:S(2)}, u32[]{:S(2)}) async-start(f32[8,7,2048]{2,1,0:T(8,128)} %reshape.234), calls=%async_computation.3 | async-start | bytes 1048576 | tf_op jit(solution)/shard_map/all_to_all | solution.py:89
  82.0 4.6 %copy-start.6 = (bf16[56,768]{1,0:T(8,128)(2,1)S(1)}, bf16[56,768]{1,0:T(8,128)(2,1)}, u32[]{:S(2)}) copy-start(bf16[56,768]{1,0:T(8,128)(2,1)} %get-tuple-element.11) | copy-start | bytes 258052
  86.6 3.7 %copy-start.3 = (f32[56,768]{1,0:T(8,128)S(1)}, f32[56,768]{1,0:T(8,128)}, u32[]{:S(2)}) copy-start(f32[56,768]{1,0:T(8,128)} %fusion.6) | copy-start | bytes 516100
  86.6 3.7 %copy-start.4 = (bf16[56,2048]{1,0:T(8,128)(2,1)S(1)}, bf16[56,2048]{1,0:T(8,128)(2,1)}, u32[]{:S(2)}) copy-start(bf16[56,2048]{1,0:T(8,128)(2,1)} %reshape.231) | copy-start | bytes 688132
  90.3 8.1 %copy-start.9 = (s32[56]{0:T(128)S(1)}, s32[56]{0:T(128)}, u32[]{:S(2)}) copy-start(s32[56]{0:T(128)} %copy-done.8) | copy-start | bytes 676
where the time goes:
time: 113 us; the launch traced here: 112 us
  starting transfers between devices  25.7 us (23%)
  local copies, waits for them, and re-layouts  23.5 us (21%)
  matrix products  23.2 us (21%)
  blocking collectives  21.7 us (19%)
  waiting for transfers between devices  12.7 us (11%)
  other arithmetic  3.6 us (3%)
  between operations  1.45 us (1%)
    unnamed x1, blocking collectives  10.9 us
    all_to_all x1, waiting for transfers between devices, local(): lax.all_to_all(outbox_x, 'node', split_axis=0, concat_axis=0, tiled=True)  7.58 us
    all_to_all x1, starting transfers between devices, local(): lax.all_to_all(outbox_p, 'node', split_axis=0, concat_axis=0, tiled=True)  7.28 us
    all_to_all x1, starting transfers between devices, local(): lax.all_to_all(outbox_x, 'node', split_axis=0, concat_axis=0, tiled=True)  6 us
    all_gather x1, blocking collectives, local(): lax.all_gather(grad_out, 'local', axis=0, tiled=True)  5.41 us
    all_gather x1, blocking collectives, local(): lax.all_gather(tok_x, 'local', axis=0, tiled=True)  5.39 us
    all_to_all x1, starting transfers between devices, local(): lax.all_to_all(input_grad.reshape(node_count, CAPN, model_width), 'node',...  4.83 us
    dot_general x1, matrix products, owner_grads(): lax.dot_general(d_up, owner_x, contract_first, preferred_element_type=jnp...  4.63 us
  transfers between devices with their start and end apart: 5, of which 3 were waited for; matrix products, arithmetic and copies ran while one was open for 29% of the time, Pallas kernels for 0%

commit v1 on v0

--- a/solution.py
+++ b/solution.py
@@ -1,10 +1,15 @@
+import functools
+
 import jax
 import jax.numpy as jnp
 from jax import lax
+from jax.experimental import pallas as pl
+from jax.experimental.pallas import tpu as pltpu
 from jax.sharding import PartitionSpec as P
 
 EXP_NODE = 4
 CAPN = 7
+MESH = pl.DeviceIdType.MESH
 
 
 contract_last = (((1,), (1,)), ((), ()))
@@ -122,6 +127,426 @@
     )
 
 
+LANES = 128
+PIECE = 16
+DENSE_TOKENS = 64
+
+
+def one_hot_rows(source, width):
+    columns = lax.broadcasted_iota(jnp.int32, (source.shape[0], width), 1)
+    return jnp.where(columns == source, 1.0, 0.0).astype(jnp.bfloat16)
+
+
+def exchange_kernel(
+    node_count,
+    local_count,
+    tok_ref,
+    grad_ref,
+    ids_ref,
+    slots_ref,
+    probs_ref,
+    gate_hbm,
+    up_hbm,
+    down_hbm,
+    x_ref,
+    d_ref,
+    dgate_ref,
+    dup_ref,
+    scaled_ref,
+    gx_ref,
+    gp_ref,
+    gate_w,
+    up_w,
+    down_w,
+    pieces,
+    order,
+    total,
+    out_local,
+    in_local,
+    out_node,
+    in_node,
+    weight_sem,
+    send_sem,
+    piece_sem,
+    local_send_sem,
+    local_recv_sem,
+    node_send_sem,
+    node_recv_sem,
+):
+    f32, bf16 = jnp.float32, jnp.bfloat16
+    node, place = lax.axis_index("node"), lax.axis_index("local")
+    experts = node_count * EXP_NODE
+    expert = node * local_count + place
+    own, width = tok_ref.shape
+    tokens = node_count * local_count * own
+    chunks, chunk = gate_w.shape[0], gate_w.shape[1]
+    quarters = PIECE // (2 * own)
+    span = width // quarters
+    eighths = PIECE // own
+    fine = width // eighths
+
+    loads = []
+    for c in range(chunks):
+        for w, (source, target) in enumerate(
+            ((gate_hbm, gate_w), (up_hbm, up_w), (down_hbm, down_w))
+        ):
+            copy = pltpu.make_async_copy(
+                source.at[0, pl.ds(c * chunk, chunk), :], target.at[c], weight_sem.at[w, c]
+            )
+            copy.start()
+            loads.append(copy)
+
+    barrier = pltpu.get_barrier_semaphore()
+    for step in range(1, node_count):
+        pl.semaphore_signal(
+            barrier,
+            inc=1,
+            device_id=(lax.rem(node + step, node_count), place),
+            device_id_type=MESH,
+        )
+    for step in range(1, local_count):
+        pl.semaphore_signal(
+            barrier,
+            inc=1,
+            device_id=(node, lax.rem(place + step, local_count)),
+            device_id_type=MESH,
+        )
+
+    kept_ids = jnp.where(slots_ref[...] < CAPN, ids_ref[...], -1)
+    probs = probs_ref[...].astype(f32)
+    node_tokens, top = kept_ids.shape
+    lane = lax.broadcasted_iota(jnp.int32, (node_tokens, LANES), 1)
+    dense = jnp.zeros((node_tokens, LANES), f32)
+    for k in range(top):
+        dense = dense + jnp.where(lane == kept_ids[:, k : k + 1], probs[:, k : k + 1], 0.0)
+    token_row = lax.broadcasted_iota(jnp.int32, (node_tokens, LANES), 0)
+    row = lax.broadcasted_iota(jnp.int32, (PIECE, span), 0)
+    row_p = lax.broadcasted_iota(jnp.int32, (PIECE, LANES), 0)
+    packed = jnp.zeros((PIECE, span), f32)
+    packed_p = jnp.zeros((PIECE, LANES), f32)
+    for which, source in enumerate((tok_ref, grad_ref)):
+        rows = source[...].astype(f32)
+        for t in range(own):
+            for q in range(quarters):
+                packed = jnp.where(
+                    row == (which * own + t) * quarters + q,
+                    rows[t : t + 1, q * span : (q + 1) * span],
+                    packed,
+                )
+    for t in range(own):
+        line = jnp.sum(jnp.where(token_row == place * own + t, dense, 0.0), axis=0, keepdims=True)
+        packed_p = jnp.where(row_p == t * quarters, line, packed_p)
+    me = node * local_count + place
+    pieces[me, :, :span] = packed.astype(bf16)
+    pieces[me, :, span:] = packed_p.astype(bf16)
+
+    pl.semaphore_wait(barrier, node_count + local_count - 2)
+
+    sent = []
+
+    def send_piece(piece, target):
+        copy = pltpu.make_async_remote_copy(
+            src_ref=pieces.at[piece],
+            dst_ref=pieces.at[piece],
+            send_sem=send_sem.at[len(sent)],
+            recv_sem=piece_sem.at[piece],
+            device_id=target,
+            device_id_type=MESH,
+        )
+        copy.start()
+        sent.append(copy)
+
+    def await_piece(piece):
+        pltpu.make_async_remote_copy(
+            src_ref=pieces.at[piece],
+            dst_ref=pieces.at[piece],
+            send_sem=send_sem.at[0],
+            recv_sem=piece_sem.at[piece],
+            device_id=(node, place),
+            device_id_type=MESH,
+        ).wait_recv()
+
+    chips = local_count // 2
+    chip, core = place // 2, lax.rem(place, 2)
+    mate = (node, chip * 2 + 1 - core)
+    for step in range(1, node_count):
+        send_piece(me, (lax.rem(node + step, node_count), place))
+    for step in range(1, chips):
+        send_piece(me, (node, lax.rem(chip + step, chips) * 2 + core))
+    send_piece(me, mate)
+
+    i = lax.broadcasted_iota(jnp.int32, (order.shape[0], LANES), 0)
+    which, q, tok = i // (quarters * tokens), (i // tokens) % quarters, i % tokens
+    l, n, t = tok // (own * node_count), (tok // own) % node_count, tok % own
+    source = (n * local_count + l) * PIECE + (which * own + t) * quarters + q
+    for block in range(order.shape[1] // LANES):
+        columns = lax.broadcasted_iota(jnp.int32, (order.shape[0], LANES), 1) + block * LANES
+        order[:, block * LANES : (block + 1) * LANES] = jnp.where(
+            columns == source, 1.0, 0.0
+        ).astype(bf16)
+
+    for step in range(1, node_count):
+        piece = lax.rem(node + node_count - step, node_count) * local_count + place
+        await_piece(piece)
+        for hop in range(1, chips):
+            send_piece(piece, (node, lax.rem(chip + hop, chips) * 2 + core))
+        send_piece(piece, mate)
+    for step in range(node_count):
+        for hop in range(1, chips):
+            piece = (
+                lax.rem(node + node_count - step, node_count) * local_count
+                + lax.rem(chip + chips - hop, chips) * 2
+                + core
+            )
+            await_piece(piece)
+            send_piece(piece, mate)
+    for step in range(node_count):
+        for hop in range(chips):
+            piece = (
+                lax.rem(node + node_count - step, node_count) * local_count
+                + lax.rem(chip + chips - hop, chips) * 2
+                + 1
+                - core
+            )
+            await_piece(piece)
+
+    gathered = pieces[...].reshape(order.shape[0], span + LANES)
+    for half in range(2):
+        columns = span // 2
+        at = half * columns
+        sorted_rows = jnp.dot(
+            order[...], gathered[:, at : at + columns], preferred_element_type=f32
+        ).astype(bf16)
+        for which, target in enumerate((x_ref, d_ref)):
+            for q in range(quarters):
+                first = (which * quarters + q) * tokens
+                target[:, q * span + at : q * span + at + columns] = sorted_rows[
+                    first : first + tokens
+                ]
+    weights = jnp.dot(order[:tokens, :], gathered[:, span:], preferred_element_type=f32)
+    lane = lax.broadcasted_iota(jnp.int32, (tokens, LANES), 1)
+    p_col = jnp.sum(jnp.where(lane == expert, weights, 0.0), axis=1, keepdims=True)
+
+    contract_last = (((1,), (1,)), ((), ()))
+    pair = jnp.zeros((tokens, 1), f32)
+    for c in range(chunks):
+        for copy in loads[3 * c : 3 * c + 3]:
+            copy.wait()
+        gate_pre = lax.dot_general(
+            x_ref[...], gate_w[c], contract_last, preferred_element_type=f32
+        )
+        up_pre = lax.dot_general(x_ref[...], up_w[c], contract_last, preferred_element_type=f32)
+        back = lax.dot_general(d_ref[...], down_w[c], contract_last, preferred_element_type=f32)
+        s = jax.nn.sigmoid(gate_pre)
+        activated = gate_pre * s
+        hidden = activated * up_pre
+        pair = pair + jnp.sum(hidden * back, axis=1, keepdims=True)
+        d_hidden = p_col * back
+        d_gate = (d_hidden * up_pre * s * (1.0 + gate_pre * (1.0 - s))).astype(bf16)
+        d_up = (d_hidden * activated).astype(bf16)
+        at = pl.ds(c * chunk, chunk)
+        dgate_ref[:, at] = d_gate
+        dup_ref[:, at] = d_up
+        scaled_ref[:, at] = (p_col * hidden).astype(bf16)
+        for half in range(4):
+            columns = pl.ds(half * (width // 4), width // 4)
+            part = jnp.dot(d_gate, gate_w[c, :, columns], preferred_element_type=f32) + jnp.dot(
+                d_up, up_w[c, :, columns], preferred_element_type=f32
+            )
+            if c == 0:
+                total[:, columns] = part
+            else:
+                total[:, columns] += part
+
+    high = pair.astype(bf16).astype(f32)
+    total[:, width:] = jnp.where(
+        lane == expert, high, jnp.where(lane == expert + experts, pair - high, 0.0)
+    )
+    out_local[...] = total[...].astype(bf16).reshape(out_local.shape)
+    group = own * node_count
+    copies = []
+    for step in range(1, local_count):
+        peer = lax.rem(place + step, local_count)
+        copy = pltpu.make_async_remote_copy(
+            src_ref=out_local.at[peer],
+            dst_ref=in_local.at[place],
+            send_sem=local_send_sem.at[step],
+            recv_sem=local_recv_sem.at[place],
+            device_id=(node, peer),
+            device_id_type=MESH,
+        )
+        copy.start()
+        copies.append(copy)
+    summed = total[pl.ds(pl.multiple_of(place * group, group), group), :]
+    for step in range(1, local_count):
+        peer = lax.rem(place + local_count - step, local_count)
+        pltpu.make_async_remote_copy(
+            src_ref=out_local.at[peer],
+            dst_ref=in_local.at[peer],
+            send_sem=local_send_sem.at[0],
+            recv_sem=local_recv_sem.at[peer],
+            device_id=(node, peer),
+            device_id_type=MESH,
+        ).wait_recv()
+        summed = summed + in_local[peer].astype(f32)
+
+    summed = summed.astype(bf16)
+    count = eighths * group
+    stacked = jnp.concatenate(
+        [summed[:, e * fine : (e + 1) * fine] for e in range(eighths)], axis=0
+    )
+    i = lax.broadcasted_iota(jnp.int32, (count, 1), 0)
+    n, t, e = i // PIECE, (i // eighths) % own, i % eighths
+    spread = one_hot_rows(e * group + n * own + t, count)
+    out_node[:, :, :fine] = (
+        jnp.dot(spread, stacked, preferred_element_type=f32)
+        .astype(bf16)
+        .reshape(node_count, PIECE, fine)
+    )
+    tail = jnp.where(e == 0, n * own + t, -1)
+    out_node[:, :, fine:] = (
+        jnp.dot(one_hot_rows(tail, group), summed[:, width:], preferred_element_type=f32)
+        .astype(bf16)
+        .reshape(node_count, PIECE, LANES)
+    )
+    for step in range(1, node_count):
+        peer = lax.rem(node + step, node_count)
+        copy = pltpu.make_async_remote_copy(
+            src_ref=out_node.at[peer],
+            dst_ref=in_node.at[node],
+            send_sem=node_send_sem.at[step],
+            recv_sem=node_recv_sem.at[node],
+            device_id=(peer, place),
+            device_id_type=MESH,
+        )
+        copy.start()
+        copies.append(copy)
+    result = out_node[node].astype(f32)
+    for step in range(1, node_count):
+        peer = lax.rem(node + node_count - step, node_count)
+        pltpu.make_async_remote_copy(
+            src_ref=out_node.at[peer],
+            dst_ref=in_node.at[peer],
+            send_sem=node_send_sem.at[0],
+            recv_sem=node_recv_sem.at[peer],
+            device_id=(peer, place),
+            device_id_type=MESH,
+        ).wait_recv()
+        result = result + in_node[peer].astype(f32)
+
+    rounded = result[:, :fine].astype(bf16)
+    t8 = lax.broadcasted_iota(jnp.int32, (8, 1), 0)
+    for e in range(eighths):
+        picked = jnp.dot(
+            one_hot_rows(t8 * eighths + e, PIECE), rounded, preferred_element_type=f32
+        )
+        gx_ref[:, e * fine : (e + 1) * fine] = picked[:own].astype(bf16)
+    row = lax.broadcasted_iota(jnp.int32, (PIECE, LANES), 0)
+    token_row = lax.broadcasted_iota(jnp.int32, (node_tokens, top), 0)
+    eye = lax.broadcasted_iota(jnp.int32, (top, top), 0) == lax.broadcasted_iota(
+        jnp.int32, (top, top), 1
+    )
+    lane = lax.broadcasted_iota(jnp.int32, (top, LANES), 1).astype(f32)
+    ids_f = kept_ids.astype(f32)
+    for t in range(own):
+        line = jnp.sum(jnp.where(row == t * eighths, result[:, fine:], 0.0), axis=0, keepdims=True)
+        ids_row = jnp.sum(
+            jnp.where(token_row == place * own + t, ids_f, 0.0), axis=0, keepdims=True
+        )
+        ids_col = jnp.sum(jnp.where(eye, ids_row, 0.0), axis=1, keepdims=True)
+        hit = (ids_col >= 0.0) & ((lane == ids_col) | (lane == ids_col + experts))
+        found = jnp.sum(jnp.where(hit, line, 0.0), axis=1, keepdims=True)
+        gp_ref[t : t + 1, :] = jnp.sum(jnp.where(eye, found, 0.0), axis=0, keepdims=True)
+
+    for copy in sent:
+        copy.wait_send()
+    for copy in copies:
+        copy.wait_send()
+
+
+def outer_kernel(x_ref, d_ref, dgate_ref, dup_ref, scaled_ref, gate_ref, up_ref, down_ref):
+    contract_first = (((0,), (0,)), ((), ()))
+    for left, right, target in (
+        (dgate_ref, x_ref, gate_ref),
+        (dup_ref, x_ref, up_ref),
+        (scaled_ref, d_ref, down_ref),
+    ):
+        target[0] = lax.dot_general(
+            left[...], right[...], contract_first, preferred_element_type=jnp.float32
+        )
+
+
+def dense_local(
+    tok_x, grad_out, expert_ids, slot_ids, route_probs, gate_weight, up_weight, down_weight
+):
+    node_count, local_count = lax.axis_size("node"), lax.axis_size("local")
+    own, width = tok_x.shape
+    top = expert_ids.shape[1]
+    hidden = gate_weight.shape[1]
+    devices = node_count * local_count
+    tokens = devices * own
+    chunk = 256 if hidden % 256 == 0 else hidden
+    chunks = hidden // chunk
+    quarters = PIECE // (2 * own)
+    span = width // quarters
+    fine = width * own // PIECE
+    f32, bf16 = jnp.float32, jnp.bfloat16
+    vmem = pl.BlockSpec(memory_space=pltpu.VMEM)
+    hbm = pl.BlockSpec(memory_space=pl.ANY)
+    dma = pltpu.SemaphoreType.DMA
+    group = own * node_count
+    rows_x, rows_d, d_gate, d_up, scaled, grad_x, grad_probs = pl.pallas_call(
+        functools.partial(exchange_kernel, node_count, local_count),
+        out_shape=(
+            jax.ShapeDtypeStruct((tokens, width), bf16),
+            jax.ShapeDtypeStruct((tokens, width), bf16),
+            jax.ShapeDtypeStruct((tokens, hidden), bf16),
+            jax.ShapeDtypeStruct((tokens, hidden), bf16),
+            jax.ShapeDtypeStruct((tokens, hidden), bf16),
+            jax.ShapeDtypeStruct((own, width), bf16),
+            jax.ShapeDtypeStruct((own, top), f32),
+        ),
+        in_specs=[vmem] * 5 + [hbm] * 3,
+        out_specs=(vmem,) * 7,
+        scratch_shapes=[
+            pltpu.VMEM((chunks, chunk, width), bf16),
+            pltpu.VMEM((chunks, chunk, width), bf16),
+            pltpu.VMEM((chunks, chunk, width), bf16),
+            pltpu.VMEM((devices, PIECE, span + LANES), bf16),
+            pltpu.VMEM((devices * PIECE, devices * PIECE), bf16),
+            pltpu.VMEM((tokens, width + LANES), f32),
+            pltpu.VMEM((local_count, group, width + LANES), bf16),
+            pltpu.VMEM((local_count, group, width + LANES), bf16),
+            pltpu.VMEM((node_count, PIECE, fine + LANES), bf16),
+            pltpu.VMEM((node_count, PIECE, fine + LANES), bf16),
+            dma((3, chunks)),
+            dma((devices,)),
+            dma((devices,)),
+            dma((local_count,)),
+            dma((local_count,)),
+            dma((node_count,)),
+            dma((node_count,)),
+        ],
+        compiler_params=pltpu.CompilerParams(
+            collective_id=0, has_side_effects=True, vmem_limit_bytes=48 * 1024 * 1024
+        ),
+    )(tok_x, grad_out, expert_ids, slot_ids, route_probs, gate_weight, up_weight, down_weight)
+    block = 128 if hidden % 128 == 0 else hidden
+    grad = jax.ShapeDtypeStruct((1, hidden, width), f32)
+    whole = pl.BlockSpec((tokens, width), lambda i: (0, 0))
+    part = pl.BlockSpec((tokens, block), lambda i: (0, i))
+    out = pl.BlockSpec((1, block, width), lambda i: (0, i, 0))
+    gate_grad, up_grad, down_grad = pl.pallas_call(
+        outer_kernel,
+        out_shape=(grad, grad, grad),
+        grid=(hidden // block,),
+        in_specs=[whole, whole, part, part, part],
+        out_specs=(out, out, out),
+        compiler_params=pltpu.CompilerParams(vmem_limit_bytes=32 * 1024 * 1024),
+    )(rows_x, rows_d, d_gate, d_up, scaled)
+    return grad_x, grad_probs, gate_grad, up_grad, down_grad
+
+
 def solution(mesh):
     in_specs = (
         P(("node", "local"), None),
@@ -140,4 +565,15 @@
         P(("node", "local"), None, None),
         P(("node", "local"), None, None),
     )
-    return jax.shard_map(local, mesh=mesh, in_specs=in_specs, out_specs=out_specs, check_vma=False)
+    node_count, local_count = mesh.shape["node"], mesh.shape["local"]
+
+    def step(*args):
+        tokens = args[0].shape[0] * node_count * local_count
+        dense = (
+            tokens <= DENSE_TOKENS
+            and local_count == EXP_NODE
+            and 2 * EXP_NODE * node_count <= LANES
+        )
+        return (dense_local if dense else local)(*args)
+
+    return jax.shard_map(step, mesh=mesh, in_specs=in_specs, out_specs=out_specs, check_vma=False)

time: 113 us -> 46 us (0.41)
  Pallas kernels: 0 us -> 38.5 us
  starting transfers between devices: 25.7 us -> 0 us
  matrix products: 23.2 us -> 0 us
  blocking collectives: 21.7 us -> 0 us
  local copies, waits for them, and re-layouts: 23.5 us -> 6.49 us
  waiting for transfers between devices: 12.7 us -> 0 us
  other arithmetic: 3.6 us -> 0 us
    pallas_call x0 -> x2, Pallas kernels: none -> 38.5 us  [the longest x1 31.2 us: dense_local(): pl.pallas_call(functools.partial(exchange_kernel, node_count, local_count...]
    all_to_all x5 -> x0, starting transfers between devices: 25.7 us -> none  [the longest x1 7.28 us: local(): lax.all_to_all(outbox_p, 'node', split_axis=0, concat_axis=0, tiled=True)]
    dot_general x9 -> x0, matrix products: 23.2 us -> none  [the longest x1 4.63 us: owner_grads(): lax.dot_general(d_up, owner_x, contract_first, preferred_element_type=jnp...]
    all_to_all x5 -> x0, waiting for transfers between devices: 12.7 us -> none  [the longest x1 7.58 us: local(): lax.all_to_all(outbox_x, 'node', split_axis=0, concat_axis=0, tiled=True)]
    reshape x11 -> x0, local copies, waits for them, and re-layouts: 12.6 us -> none  [the longest x1 1.89 us: local(): back_x.reshape(-1, model_width)]
    unnamed x1 -> x0, blocking collectives: 10.9 us -> none
    all_gather x2 -> x0, blocking collectives: 10.8 us -> none  [the longest x1 5.41 us: local(): lax.all_gather(grad_out, 'local', axis=0, tiled=True)]
    gather x3 -> x0, local copies, waits for them, and re-layouts: 2.91 us -> none  [the longest x1 1.41 us: local(): jnp.take(node_x, token_rows, axis=0, mode='fill', fill_value=0)]
  transfers between devices with their start and end apart: 5 -> 0, of which waited for: 3 -> 0; matrix products, arithmetic and copies ran while one was open for 29% -> 0% of each run, Pallas kernels for 0% -> 0%
where the time goes in v1:
time: 46 us; the launch traced here: 45.7 us
  Pallas kernels  38.5 us (84%)
  local copies, waits for them, and re-layouts  6.49 us (14%)
  between operations  0.66 us (1%)
    pallas_call x1, Pallas kernels, dense_local(): pl.pallas_call(functools.partial(exchange_kernel, node_count, local_count...  31.2 us
    pallas_call x1, Pallas kernels, dense_local(): pl.pallas_call(outer_kernel, out_shape=(grad, grad, grad), grid=(hidden /...  7.32 us
    unnamed x14, local copies, waits for them, and re-layouts  6.49 us

profile of v1, /device:TPU:0, one launch (start us, length us, event | category | flops | bytes accessed | tf_op | source)
XLA Modules:
  0.0 45.7 jit_solution(17599046908513457537)
XLA Ops:
  0.6 0.0 copy-start
  0.6 1.9 %copy-done = bf16[1,768,2048]{2,1,0:T(8,128)(2,1)S(1)} copy-done((bf16[1,768,2048]{2,1,0:T(8,128)(2,1)S(1)}, bf16[1,768,2048]{2,1,0:T(8,128)(2,1)}, u32[]{:S(2)}) %copy-start) | copy-done | bytes 3145752
  2.5 0.0 copy-start.1
  2.5 0.7 %copy-done.1 = bf16[2,2048]{1,0:T(2,128)(2,1)S(1)} copy-done((bf16[2,2048]{1,0:T(2,128)(2,1)S(1)}, bf16[2,2048]{1,0:T(2,128)(2,1)}, u32[]{:S(2)}) %copy-start.1) | copy-done | bytes 8216
  3.2 0.0 copy-start.2
  3.2 0.7 %copy-done.2 = bf16[2,2048]{1,0:T(2,128)(2,1)S(1)} copy-done((bf16[2,2048]{1,0:T(2,128)(2,1)S(1)}, bf16[2,2048]{1,0:T(2,128)(2,1)}, u32[]{:S(2)}) %copy-start.2) | copy-done | bytes 8216
  3.9 0.0 copy-start.3
  3.9 0.7 %copy-done.3 = s32[8,8]{1,0:T(8,128)S(1)} copy-done((s32[8,8]{1,0:T(8,128)S(1)}, s32[8,8]{1,0:T(8,128)}, u32[]{:S(2)}) %copy-start.3) | copy-done | bytes 280
  4.6 0.0 copy-start.4
  4.6 0.7 %copy-done.4 = s32[8,8]{1,0:T(8,128)S(1)} copy-done((s32[8,8]{1,0:T(8,128)S(1)}, s32[8,8]{1,0:T(8,128)}, u32[]{:S(2)}) %copy-start.4) | copy-done | bytes 280
  5.3 0.0 copy-start.5
  5.3 0.7 %copy-done.5 = bf16[8,8]{1,0:T(8,128)(2,1)S(1)} copy-done((bf16[8,8]{1,0:T(8,128)(2,1)S(1)}, bf16[8,8]{1,0:T(8,128)(2,1)}, u32[]{:S(2)}) %copy-start.5) | copy-done | bytes 152
  6.0 31.2 %shard_map.119 = (bf16[64,2048]{1,0:T(8,128)(2,1)S(1)}, bf16[64,2048]{1,0:T(8,128)(2,1)S(1)}, bf16[64,768]{1,0:T(8,128)(2,1)S(1)}, bf16[64,768]{1,0:T(8,128)(2,1...) custom-call(bf16[2,2048]{1,0:T(2,128)(2,1)S(1)} %copy-done.1, ...), custom_call_target="tpu_custom_call" | custom-call | tf_op jit(solution)/shard_map/pallas_call | solution.py:498
  37.2 7.3 %shard_map.120 = (f32[1,768,2048]{2,1,0:T(8,128)}, f32[1,768,2048]{2,1,0:T(8,128)}, f32[1,768,2048]{2,1,0:T(8,128)}) custom-call(bf16[64,2048]{1,0:T(8,128)(2,1)S(1)} %get-tuple-element.17.x_ref, bf16[64,2048]{1,0:T(8,128)(2,1)S(1)} %get-tuple-element.18.d_ref, bf16[64,768]{1,0:T(8,128)(2,1)S(1)} %get-tuple-element.19.dgate_ref, ...), custom_call_target="tpu_custom_call" | custom-call | tf_op jit(solution)/shard_map/pallas_call | solution.py:539
  44.5 0.6 %copy.15 = bf16[2,2048]{1,0:T(2,128)(2,1)} copy(bf16[2,2048]{1,0:T(2,128)(2,1)S(1)} %get-tuple-element.30) | data formatting | bytes 16384
  45.1 0.6 %copy.16 = f32[2,8]{1,0:T(2,128)} copy(f32[2,8]{1,0:T(2,128)S(1)} %get-tuple-element.31) | data formatting | bytes 128
Async XLA Ops:
  0.6 1.9 %copy-start = (bf16[1,768,2048]{2,1,0:T(8,128)(2,1)S(1)}, bf16[1,768,2048]{2,1,0:T(8,128)(2,1)}, u32[]{:S(2)}) copy-start(bf16[1,768,2048]{2,1,0:T(8,128)(2,1)} %gate_hbm.1) | copy-start | bytes 9437188
  2.5 0.7 %copy-start.1 = (bf16[2,2048]{1,0:T(2,128)(2,1)S(1)}, bf16[2,2048]{1,0:T(2,128)(2,1)}, u32[]{:S(2)}) copy-start(bf16[2,2048]{1,0:T(2,128)(2,1)} %tok_ref.1) | copy-start | bytes 24580
  3.2 0.7 %copy-start.2 = (bf16[2,2048]{1,0:T(2,128)(2,1)S(1)}, bf16[2,2048]{1,0:T(2,128)(2,1)}, u32[]{:S(2)}) copy-start(bf16[2,2048]{1,0:T(2,128)(2,1)} %grad_ref.1) | copy-start | bytes 24580
  3.9 0.7 %copy-start.3 = (s32[8,8]{1,0:T(8,128)S(1)}, s32[8,8]{1,0:T(8,128)}, u32[]{:S(2)}) copy-start(s32[8,8]{1,0:T(8,128)} %ids_ref.1) | copy-start | bytes 772
  4.6 0.7 %copy-start.4 = (s32[8,8]{1,0:T(8,128)S(1)}, s32[8,8]{1,0:T(8,128)}, u32[]{:S(2)}) copy-start(s32[8,8]{1,0:T(8,128)} %slots_ref.1) | copy-start | bytes 772
  5.3 0.7 %copy-start.5 = (bf16[8,8]{1,0:T(8,128)(2,1)S(1)}, bf16[8,8]{1,0:T(8,128)(2,1)}, u32[]{:S(2)}) copy-start(bf16[8,8]{1,0:T(8,128)(2,1)} %probs_ref.1) | copy-start | bytes 388

commit v2 on v1

--- a/solution.py
+++ b/solution.py
@@ -140,11 +140,11 @@
 def exchange_kernel(
     node_count,
     local_count,
-    tok_ref,
-    grad_ref,
-    ids_ref,
-    slots_ref,
-    probs_ref,
+    tok_hbm,
+    grad_hbm,
+    ids_hbm,
+    slots_hbm,
+    probs_hbm,
     gate_hbm,
     up_hbm,
     down_hbm,
@@ -153,21 +153,29 @@
     dgate_ref,
     dup_ref,
     scaled_ref,
-    gx_ref,
-    gp_ref,
+    tail_ref,
+    tok_ref,
+    grad_ref,
+    ids_ref,
+    slots_ref,
+    probs_ref,
     gate_w,
     up_w,
     down_w,
     pieces,
+    probs_node,
     order,
     total,
     out_local,
     in_local,
     out_node,
     in_node,
+    small_sem,
     weight_sem,
     send_sem,
     piece_sem,
+    prob_send_sem,
+    prob_recv_sem,
     local_send_sem,
     local_recv_sem,
     node_send_sem,
@@ -179,19 +187,36 @@
     expert = node * local_count + place
     own, width = tok_ref.shape
     tokens = node_count * local_count * own
-    chunks, chunk = gate_w.shape[0], gate_w.shape[1]
+    hidden_units = gate_w.shape[0]
+    chunks = weight_sem.shape[1]
+    chunk = hidden_units // chunks
+    halves = out_local.shape[0]
+    piece_width = width // halves
     quarters = PIECE // (2 * own)
     span = width // quarters
     eighths = PIECE // own
-    fine = width // eighths
-
+    fine = piece_width // eighths
+
+    small = []
+    for index, (source, target) in enumerate(
+        (
+            (tok_hbm, tok_ref),
+            (grad_hbm, grad_ref),
+            (ids_hbm, ids_ref),
+            (slots_hbm, slots_ref),
+            (probs_hbm, probs_ref),
+        )
+    ):
+        copy = pltpu.make_async_copy(source, target, small_sem.at[index])
+        copy.start()
+        small.append(copy)
     loads = []
     for c in range(chunks):
         for w, (source, target) in enumerate(
             ((gate_hbm, gate_w), (up_hbm, up_w), (down_hbm, down_w))
         ):
             copy = pltpu.make_async_copy(
-                source.at[0, pl.ds(c * chunk, chunk), :], target.at[c], weight_sem.at[w, c]
+                source.at[0, pl.ds(c * chunk, chunk), :], target.at[pl.ds(c * chunk, chunk), :], weight_sem.at[w, c]
             )
             copy.start()
             loads.append(copy)
@@ -212,6 +237,8 @@
             device_id_type=MESH,
         )
 
+    for copy in small:
+        copy.wait()
     kept_ids = jnp.where(slots_ref[...] < CAPN, ids_ref[...], -1)
     probs = probs_ref[...].astype(f32)
     node_tokens, top = kept_ids.shape
@@ -219,11 +246,8 @@
     dense = jnp.zeros((node_tokens, LANES), f32)
     for k in range(top):
         dense = dense + jnp.where(lane == kept_ids[:, k : k + 1], probs[:, k : k + 1], 0.0)
-    token_row = lax.broadcasted_iota(jnp.int32, (node_tokens, LANES), 0)
     row = lax.broadcasted_iota(jnp.int32, (PIECE, span), 0)
-    row_p = lax.broadcasted_iota(jnp.int32, (PIECE, LANES), 0)
     packed = jnp.zeros((PIECE, span), f32)
-    packed_p = jnp.zeros((PIECE, LANES), f32)
     for which, source in enumerate((tok_ref, grad_ref)):
         rows = source[...].astype(f32)
         for t in range(own):
@@ -233,12 +257,11 @@
                     rows[t : t + 1, q * span : (q + 1) * span],
                     packed,
                 )
-    for t in range(own):
-        line = jnp.sum(jnp.where(token_row == place * own + t, dense, 0.0), axis=0, keepdims=True)
-        packed_p = jnp.where(row_p == t * quarters, line, packed_p)
     me = node * local_count + place
-    pieces[me, :, :span] = packed.astype(bf16)
-    pieces[me, :, span:] = packed_p.astype(bf16)
+    pieces[me] = packed.astype(bf16)
+    probs_node[node] = jnp.concatenate(
+        [dense, jnp.zeros((PIECE - node_tokens, LANES), f32)], axis=0
+    ).astype(bf16)
 
     pl.semaphore_wait(barrier, node_count + local_count - 2)
 
@@ -274,6 +297,18 @@
     for step in range(1, chips):
         send_piece(me, (node, lax.rem(chip + step, chips) * 2 + core))
     send_piece(me, mate)
+    copies = []
+    for step in range(1, node_count):
+        copy = pltpu.make_async_remote_copy(
+            src_ref=probs_node.at[node],
+            dst_ref=probs_node.at[node],
+            send_sem=prob_send_sem.at[step],
+            recv_sem=prob_recv_sem.at[node],
+            device_id=(lax.rem(node + step, node_count), place),
+            device_id_type=MESH,
+        )
+        copy.start()
+        copies.append(copy)
 
     i = lax.broadcasted_iota(jnp.int32, (order.shape[0], LANES), 0)
     which, q, tok = i // (quarters * tokens), (i // tokens) % quarters, i % tokens
@@ -284,6 +319,23 @@
         order[:, block * LANES : (block + 1) * LANES] = jnp.where(
             columns == source, 1.0, 0.0
         ).astype(bf16)
+
+    token_row = lax.broadcasted_iota(jnp.int32, (node_tokens, top), 0)
+    eye = lax.broadcasted_iota(jnp.int32, (top, top), 0) == lax.broadcasted_iota(
+        jnp.int32, (top, top), 1
+    )
+    lane = lax.broadcasted_iota(jnp.int32, (top, LANES), 1).astype(f32)
+    ids_f = kept_ids.astype(f32)
+    for t in range(own):
+        ids_row = jnp.sum(
+            jnp.where(token_row == place * own + t, ids_f, 0.0), axis=0, keepdims=True
+        )
+        ids_col = jnp.sum(jnp.where(eye, ids_row, 0.0), axis=1, keepdims=True)
+        hit = (ids_col >= 0.0) & ((lane == ids_col) | (lane == ids_col + experts))
+        tail_ref[halves + 1, t * top : (t + 1) * top, :] = jnp.where(hit, 1.0, 0.0)
+    i = lax.broadcasted_iota(jnp.int32, (tokens, 1), 0)
+    l, n, t = i // (own * node_count), (i // own) % node_count, i % own
+    prob_order = one_hot_rows(n * PIECE + l * own + t, node_count * PIECE)
 
     for step in range(1, node_count):
         piece = lax.rem(node + node_count - step, node_count) * local_count + place
@@ -310,7 +362,7 @@
             )
             await_piece(piece)
 
-    gathered = pieces[...].reshape(order.shape[0], span + LANES)
+    gathered = pieces[...].reshape(order.shape[0], span)
     for half in range(2):
         columns = span // 2
         at = half * columns
@@ -323,7 +375,21 @@
                 target[:, q * span + at : q * span + at + columns] = sorted_rows[
                     first : first + tokens
                 ]
-    weights = jnp.dot(order[:tokens, :], gathered[:, span:], preferred_element_type=f32)
+    for step in range(1, node_count):
+        peer = lax.rem(node + node_count - step, node_count)
+        pltpu.make_async_remote_copy(
+            src_ref=probs_node.at[peer],
+            dst_ref=probs_node.at[peer],
+            send_sem=prob_send_sem.at[0],
+            recv_sem=prob_recv_sem.at[peer],
+            device_id=(peer, place),
+            device_id_type=MESH,
+        ).wait_recv()
+    weights = jnp.dot(
+        prob_order,
+        probs_node[...].reshape(node_count * PIECE, LANES),
+        preferred_element_type=f32,
+    )
     lane = lax.broadcasted_iota(jnp.int32, (tokens, LANES), 1)
     p_col = jnp.sum(jnp.where(lane == expert, weights, 0.0), axis=1, keepdims=True)
 
@@ -332,11 +398,12 @@
     for c in range(chunks):
         for copy in loads[3 * c : 3 * c + 3]:
             copy.wait()
+        at = pl.ds(c * chunk, chunk)
         gate_pre = lax.dot_general(
-            x_ref[...], gate_w[c], contract_last, preferred_element_type=f32
-        )
-        up_pre = lax.dot_general(x_ref[...], up_w[c], contract_last, preferred_element_type=f32)
-        back = lax.dot_general(d_ref[...], down_w[c], contract_last, preferred_element_type=f32)
+            x_ref[...], gate_w[at, :], contract_last, preferred_element_type=f32
+        )
+        up_pre = lax.dot_general(x_ref[...], up_w[at, :], contract_last, preferred_element_type=f32)
+        back = lax.dot_general(d_ref[...], down_w[at, :], contract_last, preferred_element_type=f32)
         s = jax.nn.sigmoid(gate_pre)
         activated = gate_pre * s
         hidden = activated * up_pre
@@ -344,119 +411,107 @@
         d_hidden = p_col * back
         d_gate = (d_hidden * up_pre * s * (1.0 + gate_pre * (1.0 - s))).astype(bf16)
         d_up = (d_hidden * activated).astype(bf16)
-        at = pl.ds(c * chunk, chunk)
         dgate_ref[:, at] = d_gate
         dup_ref[:, at] = d_up
         scaled_ref[:, at] = (p_col * hidden).astype(bf16)
-        for half in range(4):
-            columns = pl.ds(half * (width // 4), width // 4)
-            part = jnp.dot(d_gate, gate_w[c, :, columns], preferred_element_type=f32) + jnp.dot(
-                d_up, up_w[c, :, columns], preferred_element_type=f32
-            )
-            if c == 0:
-                total[:, columns] = part
-            else:
-                total[:, columns] += part
 
     high = pair.astype(bf16).astype(f32)
-    total[:, width:] = jnp.where(
+    total[0, :, piece_width:] = jnp.where(
         lane == expert, high, jnp.where(lane == expert + experts, pair - high, 0.0)
     )
-    out_local[...] = total[...].astype(bf16).reshape(out_local.shape)
     group = own * node_count
-    copies = []
-    for step in range(1, local_count):
-        peer = lax.rem(place + step, local_count)
-        copy = pltpu.make_async_remote_copy(
-            src_ref=out_local.at[peer],
-            dst_ref=in_local.at[place],
-            send_sem=local_send_sem.at[step],
-            recv_sem=local_recv_sem.at[place],
-            device_id=(node, peer),
-            device_id_type=MESH,
-        )
-        copy.start()
-        copies.append(copy)
-    summed = total[pl.ds(pl.multiple_of(place * group, group), group), :]
-    for step in range(1, local_count):
-        peer = lax.rem(place + local_count - step, local_count)
-        pltpu.make_async_remote_copy(
-            src_ref=out_local.at[peer],
-            dst_ref=in_local.at[peer],
-            send_sem=local_send_sem.at[0],
-            recv_sem=local_recv_sem.at[peer],
-            device_id=(node, peer),
-            device_id_type=MESH,
-        ).wait_recv()
-        summed = summed + in_local[peer].astype(f32)
-
-    summed = summed.astype(bf16)
+    used = [piece_width + (LANES if half == 0 else 0) for half in range(halves)]
+    block = piece_width // 2
+    out_local[0, :, :, piece_width:] = (
+        total[0, :, piece_width:].astype(bf16).reshape(local_count, group, LANES)
+    )
+    for half in range(halves):
+        for at in range(0, piece_width, block):
+            columns = pl.ds(half * piece_width + at, block)
+            part = jnp.dot(
+                dgate_ref[...], gate_w[:, columns], preferred_element_type=f32
+            ) + jnp.dot(dup_ref[...], up_w[:, columns], preferred_element_type=f32)
+            total[half, :, at : at + block] = part
+            out_local[half, :, :, at : at + block] = part.astype(bf16).reshape(
+                local_count, group, block
+            )
+        for step in range(1, local_count):
+            peer = lax.rem(place + step, local_count)
+            copy = pltpu.make_async_remote_copy(
+                src_ref=out_local.at[half, peer, :, pl.ds(0, used[half])],
+                dst_ref=in_local.at[half, place, :, pl.ds(0, used[half])],
+                send_sem=local_send_sem.at[half, step],
+                recv_sem=local_recv_sem.at[half, place],
+                device_id=(node, peer),
+                device_id_type=MESH,
+            )
+            copy.start()
+            copies.append(copy)
+
     count = eighths * group
-    stacked = jnp.concatenate(
-        [summed[:, e * fine : (e + 1) * fine] for e in range(eighths)], axis=0
-    )
     i = lax.broadcasted_iota(jnp.int32, (count, 1), 0)
     n, t, e = i // PIECE, (i // eighths) % own, i % eighths
     spread = one_hot_rows(e * group + n * own + t, count)
-    out_node[:, :, :fine] = (
-        jnp.dot(spread, stacked, preferred_element_type=f32)
-        .astype(bf16)
-        .reshape(node_count, PIECE, fine)
-    )
-    tail = jnp.where(e == 0, n * own + t, -1)
-    out_node[:, :, fine:] = (
-        jnp.dot(one_hot_rows(tail, group), summed[:, width:], preferred_element_type=f32)
-        .astype(bf16)
-        .reshape(node_count, PIECE, LANES)
-    )
-    for step in range(1, node_count):
-        peer = lax.rem(node + step, node_count)
-        copy = pltpu.make_async_remote_copy(
-            src_ref=out_node.at[peer],
-            dst_ref=in_node.at[node],
-            send_sem=node_send_sem.at[step],
-            recv_sem=node_recv_sem.at[node],
-            device_id=(peer, place),
-            device_id_type=MESH,
-        )
-        copy.start()
-        copies.append(copy)
-    result = out_node[node].astype(f32)
-    for step in range(1, node_count):
-        peer = lax.rem(node + node_count - step, node_count)
-        pltpu.make_async_remote_copy(
-            src_ref=out_node.at[peer],
-            dst_ref=in_node.at[peer],
-            send_sem=node_send_sem.at[0],
-            recv_sem=node_recv_sem.at[peer],
-            device_id=(peer, place),
-            device_id_type=MESH,
-        ).wait_recv()
-        result = result + in_node[peer].astype(f32)
-
-    rounded = result[:, :fine].astype(bf16)
-    t8 = lax.broadcasted_iota(jnp.int32, (8, 1), 0)
-    for e in range(eighths):
-        picked = jnp.dot(
-            one_hot_rows(t8 * eighths + e, PIECE), rounded, preferred_element_type=f32
-        )
-        gx_ref[:, e * fine : (e + 1) * fine] = picked[:own].astype(bf16)
-    row = lax.broadcasted_iota(jnp.int32, (PIECE, LANES), 0)
-    token_row = lax.broadcasted_iota(jnp.int32, (node_tokens, top), 0)
-    eye = lax.broadcasted_iota(jnp.int32, (top, top), 0) == lax.broadcasted_iota(
-        jnp.int32, (top, top), 1
-    )
-    lane = lax.broadcasted_iota(jnp.int32, (top, LANES), 1).astype(f32)
-    ids_f = kept_ids.astype(f32)
-    for t in range(own):
-        line = jnp.sum(jnp.where(row == t * eighths, result[:, fine:], 0.0), axis=0, keepdims=True)
-        ids_row = jnp.sum(
-            jnp.where(token_row == place * own + t, ids_f, 0.0), axis=0, keepdims=True
-        )
-        ids_col = jnp.sum(jnp.where(eye, ids_row, 0.0), axis=1, keepdims=True)
-        hit = (ids_col >= 0.0) & ((lane == ids_col) | (lane == ids_col + experts))
-        found = jnp.sum(jnp.where(hit, line, 0.0), axis=1, keepdims=True)
-        gp_ref[t : t + 1, :] = jnp.sum(jnp.where(eye, found, 0.0), axis=0, keepdims=True)
+    spread_tail = one_hot_rows(jnp.where(e == 0, n * own + t, -1), group)
+    used_node = [fine + (LANES if half == 0 else 0) for half in range(halves)]
+    for half in range(halves):
+        summed = total[
+            half, pl.ds(pl.multiple_of(place * group, group), group), : used[half]
+        ]
+        for step in range(1, local_count):
+            peer = lax.rem(place + local_count - step, local_count)
+            pltpu.make_async_remote_copy(
+                src_ref=out_local.at[half, peer, :, pl.ds(0, used[half])],
+                dst_ref=in_local.at[half, peer, :, pl.ds(0, used[half])],
+                send_sem=local_send_sem.at[half, 0],
+                recv_sem=local_recv_sem.at[half, peer],
+                device_id=(node, peer),
+                device_id_type=MESH,
+            ).wait_recv()
+            summed = summed + in_local[half, peer, :, : used[half]].astype(f32)
+        summed = summed.astype(bf16)
+        stacked = jnp.concatenate(
+            [summed[:, e * fine : (e + 1) * fine] for e in range(eighths)], axis=0
+        )
+        out_node[half, :, :, :fine] = (
+            jnp.dot(spread, stacked, preferred_element_type=f32)
+            .astype(bf16)
+            .reshape(node_count, PIECE, fine)
+        )
+        if half == 0:
+            out_node[half, :, :, fine:] = (
+                jnp.dot(spread_tail, summed[:, piece_width:], preferred_element_type=f32)
+                .astype(bf16)
+                .reshape(node_count, PIECE, LANES)
+            )
+        for step in range(1, node_count):
+            peer = lax.rem(node + step, node_count)
+            copy = pltpu.make_async_remote_copy(
+                src_ref=out_node.at[half, peer, :, pl.ds(0, used_node[half])],
+                dst_ref=in_node.at[half, node, :, pl.ds(0, used_node[half])],
+                send_sem=node_send_sem.at[half, step],
+                recv_sem=node_recv_sem.at[half, node],
+                device_id=(peer, place),
+                device_id_type=MESH,
+            )
+            copy.start()
+            copies.append(copy)
+    for half in range(halves):
+        result = out_node[half, node, :, : used_node[half]].astype(f32)
+        for step in range(1, node_count):
+            peer = lax.rem(node + node_count - step, node_count)
+            pltpu.make_async_remote_copy(
+                src_ref=out_node.at[half, peer, :, pl.ds(0, used_node[half])],
+                dst_ref=in_node.at[half, peer, :, pl.ds(0, used_node[half])],
+                send_sem=node_send_sem.at[half, 0],
+                recv_sem=node_recv_sem.at[half, peer],
+                device_id=(peer, place),
+                device_id_type=MESH,
+            ).wait_recv()
+            result = result + in_node[half, peer, :, : used_node[half]].astype(f32)
+        tail_ref[half, :, :] = result[:, :fine]
+        if half == 0:
+            tail_ref[halves, :, :] = result[:, fine:]
 
     for copy in sent:
         copy.wait_send()
@@ -464,16 +519,65 @@
         copy.wait_send()
 
 
-def outer_kernel(x_ref, d_ref, dgate_ref, dup_ref, scaled_ref, gate_ref, up_ref, down_ref):
+def outer_kernel(
+    x_ref,
+    d_ref,
+    dgate_ref,
+    dup_ref,
+    scaled_ref,
+    tail_ref,
+    gx_ref,
+    gp_ref,
+    gate_hbm,
+    up_hbm,
+    down_hbm,
+    blocks,
+    block_sem,
+):
     contract_first = (((0,), (0,)), ((), ()))
-    for left, right, target in (
-        (dgate_ref, x_ref, gate_ref),
-        (dup_ref, x_ref, up_ref),
-        (scaled_ref, d_ref, down_ref),
-    ):
-        target[0] = lax.dot_general(
-            left[...], right[...], contract_first, preferred_element_type=jnp.float32
-        )
+    steps, block = blocks.shape[1], blocks.shape[2]
+    work = ((dgate_ref, x_ref, gate_hbm), (dup_ref, x_ref, up_hbm), (scaled_ref, d_ref, down_hbm))
+
+    def copy_of(w, step):
+        rows = pl.ds(pl.multiple_of(step * block, block), block)
+        return pltpu.make_async_copy(
+            blocks.at[w, step], work[w][2].at[0, rows, :], block_sem.at[w, step]
+        )
+
+    for step in range(steps):
+        for w, (left, right, target) in enumerate(work):
+            blocks[w, step] = lax.dot_general(
+                left[:, step * block : (step + 1) * block],
+                right[...],
+                contract_first,
+                preferred_element_type=jnp.float32,
+            )
+            copy_of(w, step).start()
+
+    halves = tail_ref.shape[0] - 2
+    own, top = gp_ref.shape
+    eighths, fine = PIECE // own, tail_ref.shape[2]
+    for t in range(own):
+        gx_ref[t : t + 1, :] = jnp.concatenate(
+            [
+                tail_ref[half, t * eighths + e : t * eighths + e + 1, :]
+                for half in range(halves)
+                for e in range(eighths)
+            ],
+            axis=1,
+        ).astype(jnp.bfloat16)
+    eye = lax.broadcasted_iota(jnp.int32, (top, top), 0) == lax.broadcasted_iota(
+        jnp.int32, (top, top), 1
+    )
+    for t in range(own):
+        line = tail_ref[halves, t * eighths : t * eighths + 1, :]
+        hit = tail_ref[halves + 1, t * top : (t + 1) * top, :]
+        found = jnp.sum(jnp.where(hit > 0.5, line, 0.0), axis=1, keepdims=True)
+        gp_ref[t : t + 1, :] = jnp.sum(jnp.where(eye, found, 0.0), axis=0, keepdims=True)
+
+    for step in range(steps):
+        for w in range(3):
+            copy_of(w, step).wait()
 
 
 def dense_local(
@@ -489,13 +593,14 @@
     chunks = hidden // chunk
     quarters = PIECE // (2 * own)
     span = width // quarters
-    fine = width * own // PIECE
+    halves = 2
+    fine = width * own // (PIECE * halves)
     f32, bf16 = jnp.float32, jnp.bfloat16
     vmem = pl.BlockSpec(memory_space=pltpu.VMEM)
-    hbm = pl.BlockSpec(memory_space=pl.ANY)
+    hbm = pl.BlockSpec(memory_space=pltpu.HBM)
     dma = pltpu.SemaphoreType.DMA
     group = own * node_count
-    rows_x, rows_d, d_gate, d_up, scaled, grad_x, grad_probs = pl.pallas_call(
+    rows_x, rows_d, d_gate, d_up, scaled, tail = pl.pallas_call(
         functools.partial(exchange_kernel, node_count, local_count),
         out_shape=(
             jax.ShapeDtypeStruct((tokens, width), bf16),
@@ -503,29 +608,37 @@
             jax.ShapeDtypeStruct((tokens, hidden), bf16),
             jax.ShapeDtypeStruct((tokens, hidden), bf16),
             jax.ShapeDtypeStruct((tokens, hidden), bf16),
-            jax.ShapeDtypeStruct((own, width), bf16),
-            jax.ShapeDtypeStruct((own, top), f32),
+            jax.ShapeDtypeStruct((halves + 2, PIECE, fine), f32),
         ),
-        in_specs=[vmem] * 5 + [hbm] * 3,
-        out_specs=(vmem,) * 7,
+        in_specs=[hbm] * 8,
+        out_specs=(vmem,) * 6,
         scratch_shapes=[
-            pltpu.VMEM((chunks, chunk, width), bf16),
-            pltpu.VMEM((chunks, chunk, width), bf16),
-            pltpu.VMEM((chunks, chunk, width), bf16),
-            pltpu.VMEM((devices, PIECE, span + LANES), bf16),
+            pltpu.VMEM(tok_x.shape, bf16),
+            pltpu.VMEM(grad_out.shape, bf16),
+            pltpu.VMEM(expert_ids.shape, expert_ids.dtype),
+            pltpu.VMEM(slot_ids.shape, slot_ids.dtype),
+            pltpu.VMEM(route_probs.shape, bf16),
+            pltpu.VMEM((hidden, width), bf16),
+            pltpu.VMEM((hidden, width), bf16),
+            pltpu.VMEM((hidden, width), bf16),
+            pltpu.VMEM((devices, PIECE, span), bf16),
+            pltpu.VMEM((node_count, PIECE, LANES), bf16),
             pltpu.VMEM((devices * PIECE, devices * PIECE), bf16),
-            pltpu.VMEM((tokens, width + LANES), f32),
-            pltpu.VMEM((local_count, group, width + LANES), bf16),
-            pltpu.VMEM((local_count, group, width + LANES), bf16),
-            pltpu.VMEM((node_count, PIECE, fine + LANES), bf16),
-            pltpu.VMEM((node_count, PIECE, fine + LANES), bf16),
+            pltpu.VMEM((halves, tokens, width // halves + LANES), f32),
+            pltpu.VMEM((halves, local_count, group, width // halves + LANES), bf16),
+            pltpu.VMEM((halves, local_count, group, width // halves + LANES), bf16),
+            pltpu.VMEM((halves, node_count, PIECE, fine + LANES), bf16),
+            pltpu.VMEM((halves, node_count, PIECE, fine + LANES), bf16),
+            dma((5,)),
             dma((3, chunks)),
             dma((devices,)),
             dma((devices,)),
-            dma((local_count,)),
-            dma((local_count,)),
             dma((node_count,)),
             dma((node_count,)),
+            dma((halves, local_count)),
+            dma((halves, local_count)),
+            dma((halves, node_count)),
+            dma((halves, node_count)),
         ],
         compiler_params=pltpu.CompilerParams(
             collective_id=0, has_side_effects=True, vmem_limit_bytes=48 * 1024 * 1024
@@ -533,17 +646,21 @@
     )(tok_x, grad_out, expert_ids, slot_ids, route_probs, gate_weight, up_weight, down_weight)
     block = 128 if hidden % 128 == 0 else hidden
     grad = jax.ShapeDtypeStruct((1, hidden, width), f32)
-    whole = pl.BlockSpec((tokens, width), lambda i: (0, 0))
-    part = pl.BlockSpec((tokens, block), lambda i: (0, i))
-    out = pl.BlockSpec((1, block, width), lambda i: (0, i, 0))
-    gate_grad, up_grad, down_grad = pl.pallas_call(
+    steps = hidden // block
+    grad_x, grad_probs, gate_grad, up_grad, down_grad = pl.pallas_call(
         outer_kernel,
-        out_shape=(grad, grad, grad),
-        grid=(hidden // block,),
-        in_specs=[whole, whole, part, part, part],
-        out_specs=(out, out, out),
-        compiler_params=pltpu.CompilerParams(vmem_limit_bytes=32 * 1024 * 1024),
-    )(rows_x, rows_d, d_gate, d_up, scaled)
+        out_shape=(
+            jax.ShapeDtypeStruct((own, width), bf16),
+            jax.ShapeDtypeStruct((own, top), f32),
+            grad,
+            grad,
+            grad,
+        ),
+        in_specs=[vmem] * 6,
+        out_specs=(vmem, vmem, hbm, hbm, hbm),
+        scratch_shapes=[pltpu.VMEM((3, steps, block, width), f32), dma((3, steps))],
+        compiler_params=pltpu.CompilerParams(vmem_limit_bytes=40 * 1024 * 1024),
+    )(rows_x, rows_d, d_gate, d_up, scaled, tail)
     return grad_x, grad_probs, gate_grad, up_grad, down_grad
 
 

time: 46 us -> 44.9 us (0.976)
  local copies, waits for them, and re-layouts: 6.49 us -> 5.33 us
    unnamed x14 -> x12, local copies, waits for them, and re-layouts: 6.49 us -> 5.33 us
where the time goes in v2:
time: 44.9 us; the launch traced here: 44.5 us
  Pallas kernels  38.6 us (86%)
  local copies, waits for them, and re-layouts  5.33 us (12%)
  between operations  0.66 us (1%)
    pallas_call x1, Pallas kernels, dense_local(): pl.pallas_call(functools.partial(exchange_kernel, node_count, local_count...  31 us
    pallas_call x1, Pallas kernels, dense_local(): pl.pallas_call(outer_kernel, out_shape=(jax.ShapeDtypeStruct((own, width)...  7.53 us
    unnamed x12, local copies, waits for them, and re-layouts  5.33 us

profile of v2, /device:TPU:0, one launch (start us, length us, event | category | flops | bytes accessed | tf_op | source)
XLA Modules:
  0.0 44.5 jit_solution(16522909213565506785)
XLA Ops:
  0.6 0.0 copy-start
  0.6 1.9 %copy-done = bf16[1,768,2048]{2,1,0:T(8,128)(2,1)S(1)} copy-done((bf16[1,768,2048]{2,1,0:T(8,128)(2,1)S(1)}, bf16[1,768,2048]{2,1,0:T(8,128)(2,1)}, u32[]{:S(2)}) %copy-start) | copy-done | bytes 3145752
  2.5 0.0 copy-start.1
  2.5 0.7 %copy-done.1 = bf16[2,2048]{1,0:T(2,128)(2,1)S(1)} copy-done((bf16[2,2048]{1,0:T(2,128)(2,1)S(1)}, bf16[2,2048]{1,0:T(2,128)(2,1)}, u32[]{:S(2)}) %copy-start.1) | copy-done | bytes 8216
  3.2 0.0 copy-start.2
  3.2 0.7 %copy-done.2 = bf16[2,2048]{1,0:T(2,128)(2,1)S(1)} copy-done((bf16[2,2048]{1,0:T(2,128)(2,1)S(1)}, bf16[2,2048]{1,0:T(2,128)(2,1)}, u32[]{:S(2)}) %copy-start.2) | copy-done | bytes 8216
  3.9 0.0 copy-start.3
  3.9 0.7 %copy-done.3 = s32[8,8]{1,0:T(8,128)S(1)} copy-done((s32[8,8]{1,0:T(8,128)S(1)}, s32[8,8]{1,0:T(8,128)}, u32[]{:S(2)}) %copy-start.3) | copy-done | bytes 280
  4.6 0.0 copy-start.4
  4.6 0.7 %copy-done.4 = s32[8,8]{1,0:T(8,128)S(1)} copy-done((s32[8,8]{1,0:T(8,128)S(1)}, s32[8,8]{1,0:T(8,128)}, u32[]{:S(2)}) %copy-start.4) | copy-done | bytes 280
  5.3 0.0 copy-start.5
  5.3 0.7 %copy-done.5 = bf16[8,8]{1,0:T(8,128)(2,1)S(1)} copy-done((bf16[8,8]{1,0:T(8,128)(2,1)S(1)}, bf16[8,8]{1,0:T(8,128)(2,1)}, u32[]{:S(2)}) %copy-start.5) | copy-done | bytes 152
  6.0 31.0 %shard_map.119 = (bf16[64,2048]{1,0:T(8,128)(2,1)S(1)}, bf16[64,2048]{1,0:T(8,128)(2,1)S(1)}, bf16[64,768]{1,0:T(8,128)(2,1)S(1)}, bf16[64,768]{1,0:T(8,128)(2,1...) custom-call(bf16[2,2048]{1,0:T(2,128)(2,1)S(1)} %copy-done.1, bf16[2,2048]{1,0:T(2,128)(2,1)S(1)} %copy-done.2, ...), custom_call_target="tpu_custom_call" | custom-call | tf_op jit(solution)/shard_map/pallas_call | solution.py:603
  37.0 7.5 %shard_map.120 = (bf16[2,2048]{1,0:T(2,128)(2,1)}, f32[2,8]{1,0:T(2,128)}, f32[1,768,2048]{2,1,0:T(8,128)}, f32[1,768,2048]{2,1,0:T(8,128)}, f32[1,768,2048]{2,1,0:T(8,128)}) custom-call(bf16[64,2048]{1,0:T(8,128)(2,1)S(1)} %get-tuple-element.11.x_ref, bf16[64,2048]{1,0:T(8,128)(2,1)S(1)} %get-tuple-element.12.d_ref, ...), custom_call_target="tpu_custom_call" | custom-call | tf_op jit(solution)/shard_map/pallas_call | solution.py:650
Async XLA Ops:
  0.6 1.9 %copy-start = (bf16[1,768,2048]{2,1,0:T(8,128)(2,1)S(1)}, bf16[1,768,2048]{2,1,0:T(8,128)(2,1)}, u32[]{:S(2)}) copy-start(bf16[1,768,2048]{2,1,0:T(8,128)(2,1)} %gate_hbm.1) | copy-start | bytes 9437188
  2.5 0.7 %copy-start.1 = (bf16[2,2048]{1,0:T(2,128)(2,1)S(1)}, bf16[2,2048]{1,0:T(2,128)(2,1)}, u32[]{:S(2)}) copy-start(bf16[2,2048]{1,0:T(2,128)(2,1)} %tok_hbm.1) | copy-start | bytes 24580
  3.2 0.7 %copy-start.2 = (bf16[2,2048]{1,0:T(2,128)(2,1)S(1)}, bf16[2,2048]{1,0:T(2,128)(2,1)}, u32[]{:S(2)}) copy-start(bf16[2,2048]{1,0:T(2,128)(2,1)} %grad_hbm.1) | copy-start | bytes 24580
  3.9 0.7 %copy-start.3 = (s32[8,8]{1,0:T(8,128)S(1)}, s32[8,8]{1,0:T(8,128)}, u32[]{:S(2)}) copy-start(s32[8,8]{1,0:T(8,128)} %ids_hbm.1) | copy-start | bytes 772
  4.6 0.7 %copy-start.4 = (s32[8,8]{1,0:T(8,128)S(1)}, s32[8,8]{1,0:T(8,128)}, u32[]{:S(2)}) copy-start(s32[8,8]{1,0:T(8,128)} %slots_hbm.1) | copy-start | bytes 772
  5.3 0.7 %copy-start.5 = (bf16[8,8]{1,0:T(8,128)(2,1)S(1)}, bf16[8,8]{1,0:T(8,128)(2,1)}, u32[]{:S(2)}) copy-start(bf16[8,8]{1,0:T(8,128)(2,1)} %probs_hbm.1) | copy-start | bytes 388

commit v3 on v2

--- a/solution.py
+++ b/solution.py
@@ -130,6 +130,7 @@
 LANES = 128
 PIECE = 16
 DENSE_TOKENS = 64
+VMEM = 64 * 1024 * 1024
 
 
 def one_hot_rows(source, width):
@@ -148,6 +149,12 @@
     gate_hbm,
     up_hbm,
     down_hbm,
+    x_hbm,
+    d_hbm,
+    dgate_hbm,
+    dup_hbm,
+    scaled_hbm,
+    tail_hbm,
     x_ref,
     d_ref,
     dgate_ref,
@@ -171,6 +178,7 @@
     out_node,
     in_node,
     small_sem,
+    store_sem,
     weight_sem,
     send_sem,
     piece_sem,
@@ -393,6 +401,15 @@
     lane = lax.broadcasted_iota(jnp.int32, (tokens, LANES), 1)
     p_col = jnp.sum(jnp.where(lane == expert, weights, 0.0), axis=1, keepdims=True)
 
+    stores = []
+
+    def store(source, target):
+        copy = pltpu.make_async_copy(source, target, store_sem.at[len(stores)])
+        copy.start()
+        stores.append(copy)
+
+    store(x_ref, x_hbm)
+    store(d_ref, d_hbm)
     contract_last = (((1,), (1,)), ((), ()))
     pair = jnp.zeros((tokens, 1), f32)
     for c in range(chunks):
@@ -415,6 +432,9 @@
         dup_ref[:, at] = d_up
         scaled_ref[:, at] = (p_col * hidden).astype(bf16)
 
+    store(dgate_ref, dgate_hbm)
+    store(dup_ref, dup_hbm)
+    store(scaled_ref, scaled_hbm)
     high = pair.astype(bf16).astype(f32)
     total[0, :, piece_width:] = jnp.where(
         lane == expert, high, jnp.where(lane == expert + experts, pair - high, 0.0)
@@ -512,30 +532,56 @@
         tail_ref[half, :, :] = result[:, :fine]
         if half == 0:
             tail_ref[halves, :, :] = result[:, fine:]
+    store(tail_ref, tail_hbm)
 
     for copy in sent:
         copy.wait_send()
     for copy in copies:
         copy.wait_send()
+    for copy in stores:
+        copy.wait()
 
 
 def outer_kernel(
+    x_hbm,
+    d_hbm,
+    dgate_hbm,
+    dup_hbm,
+    scaled_hbm,
+    tail_hbm,
+    gx_ref,
+    gp_ref,
+    gate_hbm,
+    up_hbm,
+    down_hbm,
     x_ref,
     d_ref,
     dgate_ref,
     dup_ref,
     scaled_ref,
     tail_ref,
-    gx_ref,
-    gp_ref,
-    gate_hbm,
-    up_hbm,
-    down_hbm,
     blocks,
+    load_sem,
     block_sem,
 ):
     contract_first = (((0,), (0,)), ((), ()))
-    steps, block = blocks.shape[1], blocks.shape[2]
+    steps, block, width = blocks.shape[1:]
+    loads = []
+    for index, (source, target) in enumerate(
+        (
+            (dgate_hbm, dgate_ref),
+            (x_hbm, x_ref),
+            (dup_hbm, dup_ref),
+            (scaled_hbm, scaled_ref),
+            (d_hbm, d_ref),
+            (tail_hbm, tail_ref),
+        )
+    ):
+        copy = pltpu.make_async_copy(source, target, load_sem.at[index])
+        copy.start()
+        loads.append(copy)
+    needs = (loads[:2], loads[2:3], loads[3:5])
+    tile = 256 if width % 256 == 0 else width
     work = ((dgate_ref, x_ref, gate_hbm), (dup_ref, x_ref, up_hbm), (scaled_ref, d_ref, down_hbm))
 
     def copy_of(w, step):
@@ -544,16 +590,20 @@
             blocks.at[w, step], work[w][2].at[0, rows, :], block_sem.at[w, step]
         )
 
-    for step in range(steps):
-        for w, (left, right, target) in enumerate(work):
-            blocks[w, step] = lax.dot_general(
-                left[:, step * block : (step + 1) * block],
-                right[...],
-                contract_first,
-                preferred_element_type=jnp.float32,
-            )
+    for w, (left, right, target) in enumerate(work):
+        for copy in needs[w]:
+            copy.wait()
+        for step in range(steps):
+            for at in range(0, width, tile):
+                blocks[w, step, :, at : at + tile] = lax.dot_general(
+                    left[:, step * block : (step + 1) * block],
+                    right[:, at : at + tile],
+                    contract_first,
+                    preferred_element_type=jnp.float32,
+                )
             copy_of(w, step).start()
 
+    loads[5].wait()
     halves = tail_ref.shape[0] - 2
     own, top = gp_ref.shape
     eighths, fine = PIECE // own, tail_ref.shape[2]
@@ -611,8 +661,14 @@
             jax.ShapeDtypeStruct((halves + 2, PIECE, fine), f32),
         ),
         in_specs=[hbm] * 8,
-        out_specs=(vmem,) * 6,
+        out_specs=(hbm,) * 6,
         scratch_shapes=[
+            pltpu.VMEM((tokens, width), bf16),
+            pltpu.VMEM((tokens, width), bf16),
+            pltpu.VMEM((tokens, hidden), bf16),
+            pltpu.VMEM((tokens, hidden), bf16),
+            pltpu.VMEM((tokens, hidden), bf16),
+            pltpu.VMEM((halves + 2, PIECE, fine), f32),
             pltpu.VMEM(tok_x.shape, bf16),
             pltpu.VMEM(grad_out.shape, bf16),
             pltpu.VMEM(expert_ids.shape, expert_ids.dtype),
@@ -630,6 +686,7 @@
             pltpu.VMEM((halves, node_count, PIECE, fine + LANES), bf16),
             pltpu.VMEM((halves, node_count, PIECE, fine + LANES), bf16),
             dma((5,)),
+            dma((6,)),
             dma((3, chunks)),
             dma((devices,)),
             dma((devices,)),
@@ -641,7 +698,7 @@
             dma((halves, node_count)),
         ],
         compiler_params=pltpu.CompilerParams(
-            collective_id=0, has_side_effects=True, vmem_limit_bytes=48 * 1024 * 1024
+            collective_id=0, has_side_effects=True, vmem_limit_bytes=VMEM
         ),
     )(tok_x, grad_out, expert_ids, slot_ids, route_probs, gate_weight, up_weight, down_weight)
     block = 128 if hidden % 128 == 0 else hidden
@@ -656,10 +713,20 @@
             grad,
             grad,
         ),
-        in_specs=[vmem] * 6,
+        in_specs=[hbm] * 6,
         out_specs=(vmem, vmem, hbm, hbm, hbm),
-        scratch_shapes=[pltpu.VMEM((3, steps, block, width), f32), dma((3, steps))],
-        compiler_params=pltpu.CompilerParams(vmem_limit_bytes=40 * 1024 * 1024),
+        scratch_shapes=[
+            pltpu.VMEM((tokens, width), bf16),
+            pltpu.VMEM((tokens, width), bf16),
+            pltpu.VMEM((tokens, hidden), bf16),
+            pltpu.VMEM((tokens, hidden), bf16),
+            pltpu.VMEM((tokens, hidden), bf16),
+            pltpu.VMEM((halves + 2, PIECE, fine), f32),
+            pltpu.VMEM((3, steps, block, width), f32),
+            dma((6,)),
+            dma((3, steps)),
+        ],
+        compiler_params=pltpu.CompilerParams(vmem_limit_bytes=VMEM),
     )(rows_x, rows_d, d_gate, d_up, scaled, tail)
     return grad_x, grad_probs, gate_grad, up_grad, down_grad
 

time: 44.9 us -> 40.8 us (0.909)
  local copies, waits for them, and re-layouts: 5.33 us -> 0 us
  Pallas kernels: 38.6 us -> 40 us
    unnamed x12 -> x0, local copies, waits for them, and re-layouts: 5.33 us -> none
    pallas_call x1, Pallas kernels: 7.53 us -> 8.6 us  [dense_local(): pl.pallas_call(outer_kernel, out_shape=(jax.ShapeDtypeStruct((own, width)...]
where the time goes in v3:
time: 40.8 us; the launch traced here: 40.6 us
  Pallas kernels  40 us (98%)
  between operations  0.64 us (2%)
    pallas_call x1, Pallas kernels, dense_local(): pl.pallas_call(functools.partial(exchange_kernel, node_count, local_count...  31.4 us
    pallas_call x1, Pallas kernels, dense_local(): pl.pallas_call(outer_kernel, out_shape=(jax.ShapeDtypeStruct((own, width)...  8.6 us

profile of v3, /device:TPU:0, one launch (start us, length us, event | category | flops | bytes accessed | tf_op | source)
XLA Modules:
  0.0 40.6 jit_solution(9010700560990826941)
XLA Ops:
  0.6 31.4 %shard_map.119 = (bf16[64,2048]{1,0:T(8,128)(2,1)}, bf16[64,2048]{1,0:T(8,128)(2,1)}, bf16[64,768]{1,0:T(8,128)(2,1)}, bf16[64,768]{1,0:T(8,128)(2,1)}, bf16[64,768]{1,0:T(8,128)(2,1)}, /*index=5*/f32[4,16,128]{2,1,0:T(8,128)}) custom-call(bf16[2,2048]{1,0:T(2,128)(2,1)} %tok_hbm.1, bf16[2,2048]{1,0:T(2,128)(2,1)} %grad_hbm.1, s32[8,8]{1,0:T(8,128)} %ids_hbm.1, ...), custom_call_target="tpu_custom_call" | custom-call | tf_op jit(solution)/shard_map/pallas_call | solution.py:653
  32.0 8.6 %shard_map.120 = (bf16[2,2048]{1,0:T(2,128)(2,1)}, f32[2,8]{1,0:T(2,128)}, f32[1,768,2048]{2,1,0:T(8,128)}, f32[1,768,2048]{2,1,0:T(8,128)}, f32[1,768,2048]{2,1,0:T(8,128)}) custom-call(bf16[64,2048]{1,0:T(8,128)(2,1)} %get-tuple-element.11.x_hbm, bf16[64,2048]{1,0:T(8,128)(2,1)} %get-tuple-element.12.d_hbm, bf16[64,768]{1,0:T(8,128)(2,1)} %get-tuple-element.13.dgate_hbm, ...), custom_call_target="tpu_custom_call" | custom-call | tf_op jit(solution)/shard_map/pallas_call | solution.py:707
